TPU v7x, 32 devices: a whole 2x2x4 slice. The times are simulated.
32 devices in a mesh: dom: 2 (over y), exp: 16 (over z, x, core).
Axes of the slice: x: 2, y: 2, z: 4, core: 2. Of those that a mesh axis runs over, the one named last changes fastest.
Arguments:
- queries: bfloat16 [128, 4096], P(('dom', 'exp')), parts along dimension 0
- new_keys: bfloat16 [128, 1024], P(('dom', 'exp')), parts along dimension 0, may hold values from -6 to 6
- new_values: bfloat16 [128, 1024], P(('dom', 'exp')), parts along dimension 0, may hold values from -6 to 6
- cache_keys: bfloat16 [128, 32, 1024], P(('dom', 'exp')), parts along dimension 0
- cache_values: bfloat16 [128, 32, 1024], P(('dom', 'exp')), parts along dimension 0, may hold values from -6 to 6
- lengths: int32 [128], P(('dom', 'exp')), parts along dimension 0, may hold values from 2 to 32, as said below
- norm_gain: float32 [4096], replicated, may hold values from 0.5 to 1.5
- route_ids: int32 [128, 2], P(('dom', 'exp')), parts along dimension 0, may hold values from 0 to 7, all different within a row; in each aligned block of 4 rows (0 to 3, 4 to 7, ...) at most 2 rows name the same one
- route_weights: float32 [128, 2], P(('dom', 'exp')), parts along dimension 0, may hold values from 0.1 to 1
- active_blocks: int32 [16, 64], P('dom'), parts along dimension 0, may hold values 0 or 1
- gate_weight: bfloat16 [65536, 4096], P('exp'), may hold values from -0.09375 to 0.09375
- up_weight: bfloat16 [65536, 4096], P('exp'), may hold values from -0.09375 to 0.09375
- down_weight: bfloat16 [65536, 4096], P('exp'), may hold values from -0.1875 to 0.1875
Outputs:
- attended: bfloat16 [128, 4096], P(('dom', 'exp')), parts along dimension 0
- expert_out: bfloat16 [128, 4096], P(('dom', 'exp')), parts along dimension 0
There are 2 independent parts, one for each index of `dom`. A program takes and returns all parts, laid end to end along the dimension named above; an argument that names none is the same for every part. Nothing has to cross between parts.
Inputs may be any that keep to these rules, and one draw needn't show every extreme that they name: `lengths`: the first row of the group has 32 positions in use. `route_ids`: among the rows of one device no expert is named by more than 2 rows, a bound that some block reaches.
All inputs are finite; a program needn't handle non-finite values.
Results may differ from a plain program's by a relative error of at most 0.014.
Values may be sent and summed in bfloat16 or wider, within the bound.
No kernel may reach another device: no remote copies, remote signals or barrier semaphores. Data moves between devices by JAX's collectives and lax.ppermute only.
A program may use at most 192 MiB of HBM per device.

v0:
```python
import jax
import jax.numpy as jnp
from jax import lax
from jax.sharding import PartitionSpec as P

KV_HEADS = 8
BLOCK = 128
CAP = 2


EPSILON = 1e-05


def attention(queries, new_keys, new_values, cache_keys, cache_values, lengths):
    row_count = queries.shape[0]
    query_width = queries.shape[1]
    context = cache_keys.shape[1]
    head_size = new_keys.shape[1] // KV_HEADS
    group_size = query_width // (head_size * KV_HEADS)
    query = queries.reshape(row_count, KV_HEADS, group_size, head_size)
    key_cache = cache_keys.reshape(row_count, context, KV_HEADS, head_size)
    value_cache = cache_values.reshape(row_count, context, KV_HEADS, head_size)
    own_key = new_keys.reshape(row_count, KV_HEADS, head_size)
    own_value = new_values.reshape(row_count, KV_HEADS, 1, head_size).astype(jnp.float32)
    score_scale = head_size ** (-0.5)
    cached = (
        jnp.einsum("rkgd,rpkd->rkgp", query, key_cache, preferred_element_type=jnp.float32)
        * score_scale
    )
    own_score = (
        jnp.einsum("rkgd,rkd->rkg", query, own_key, preferred_element_type=jnp.float32)
        * score_scale
    )
    valid = lax.broadcasted_iota(jnp.int32, (row_count, context), 1) < lengths[:, None]
    cached = jnp.where(valid[:, None, None, :], cached, -jnp.inf)
    row_top = jnp.maximum(jnp.max(cached, axis=3), own_score)
    cached_exp = jnp.exp(cached - row_top[..., None])
    own_exp = jnp.exp(own_score - row_top)
    denominator = jnp.sum(cached_exp, axis=3) + own_exp
    cached_prob = (cached_exp / denominator[..., None]).astype(jnp.bfloat16)
    own_prob = (own_exp / denominator).astype(jnp.bfloat16).astype(jnp.float32)
    mixture = jnp.einsum(
        "rkgp,rpkd->rkgd", cached_prob, value_cache, preferred_element_type=jnp.float32
    )
    mixture = mixture + own_prob[..., None] * own_value
    return mixture.reshape(row_count, query_width).astype(jnp.bfloat16)


def normalize(attended, norm_gain):
    features = attended.astype(jnp.float32)
    mean_square = jnp.mean(features * features, axis=1, keepdims=True)
    return (features * lax.rsqrt(mean_square + EPSILON) * norm_gain[None, :]).astype(jnp.bfloat16)


def pair_ranks(route_ids, experts):
    pair_shape = route_ids.shape
    flat_ids = route_ids.reshape(pair_shape[:-2] + (pair_shape[-2] * 2,))
    onehot = (flat_ids[..., None] == jnp.arange(experts, dtype=jnp.int32)).astype(jnp.int32)
    before = jnp.cumsum(onehot, axis=-2) - onehot
    return jnp.sum(before * onehot, axis=-1).reshape(pair_shape)


def shards(
    queries,
    new_keys,
    new_values,
    cache_keys,
    cache_values,
    lengths,
    norm_gain,
    route_ids,
    route_weights,
    active_blocks,
    gate_weight,
    up_weight,
    down_weight,
):
    devices = lax.axis_size("exp")
    experts = active_blocks.shape[0]
    groups = devices // experts
    position = lax.axis_index("exp")
    expert = position // groups
    member = position % groups
    neurons = gate_weight.shape[0]
    model_width = gate_weight.shape[1]
    attended = attention(queries, new_keys, new_values, cache_keys, cache_values, lengths)
    normed = normalize(attended, norm_gain)
    pair_rank = pair_ranks(route_ids, experts)
    expert_iota = jnp.arange(experts, dtype=jnp.int32)
    slot_iota = jnp.arange(CAP, dtype=jnp.int32)
    slot_match = (route_ids[..., None, None] == expert_iota[:, None]) & (
        pair_rank[..., None, None] == slot_iota
    )
    chooser = jnp.sum(slot_match.astype(jnp.int32), axis=1).astype(jnp.bfloat16)
    packed = jnp.einsum("rec,rd->ecd", chooser, normed, preferred_element_type=jnp.float32).astype(
        jnp.bfloat16
    )
    outgoing = jnp.repeat(packed, groups, axis=0)
    block_count = neurons // BLOCK
    expert_flags = lax.dynamic_index_in_dim(active_blocks, expert, 0, keepdims=False)
    block_flags = lax.dynamic_slice_in_dim(expert_flags, member * block_count, block_count)
    row_weights = jnp.sum(jnp.where(slot_match, route_weights[:, :, None, None], 0.0), axis=1)
    slot_rows = lax.all_to_all(outgoing, "exp", split_axis=0, concat_axis=0, tiled=True)
    flattened = slot_rows.reshape(-1, model_width)
    neuron_mask = jnp.repeat(block_flags, BLOCK).astype(jnp.float32)
    gate_value = lax.dot_general(
        flattened, gate_weight, (((1,), (1,)), ((), ())), preferred_element_type=jnp.float32
    )
    up_value = lax.dot_general(
        flattened, up_weight, (((1,), (1,)), ((), ())), preferred_element_type=jnp.float32
    )
    hidden = (jax.nn.relu(gate_value) * jax.nn.relu(up_value) * neuron_mask[None, :]).astype(
        jnp.bfloat16
    )
    partial_value = jnp.dot(hidden, down_weight, preferred_element_type=jnp.float32)
    returned = lax.all_to_all(
        partial_value.astype(jnp.bfloat16).reshape(slot_rows.shape),
        "exp",
        split_axis=0,
        concat_axis=0,
        tiled=True,
    )
    summed = jnp.sum(
        returned.reshape(experts, groups, CAP, model_width).astype(jnp.float32), axis=1
    )
    weighted = row_weights[:, :, :, None] * summed[None, :, :, :]
    expert_out = jnp.sum(weighted.reshape(weighted.shape[0], -1, model_width), axis=1)
    return (attended, expert_out.astype(jnp.bfloat16))


def solution(mesh):
    return jax.shard_map(
        shards,
        mesh=mesh,
        in_specs=(
            P(("dom", "exp"), None),
            P(("dom", "exp"), None),
            P(("dom", "exp"), None),
            P(("dom", "exp"), None, None),
            P(("dom", "exp"), None, None),
            P(("dom", "exp")),
            P(),
            P(("dom", "exp"), None),
            P(("dom", "exp"), None),
            P("dom", None),
            P("exp", None),
            P("exp", None),
            P("exp", None),
        ),
        out_specs=(P(("dom", "exp"), None), P(("dom", "exp"), None)),
        check_vma=False,
    )
```

profile of v0, /device:TPU:0, one launch (start us, length us, event | category | flops | bytes accessed | tf_op | source)
XLA Modules:
  0.0 83.3 jit_solution(16425403965413397831)
XLA Ops:
  0.6 0.8 iota_compare_fusion.1
  1.4 0.8 copy.31
  2.2 0.7 iota_compare_fusion.3
  3.1 0.2 select_reduce_fusion
  3.5 0.7 reshape.114
  4.2 0.7 convert_bitcast_fusion
  4.9 0.8 reshape.101
  5.7 0.1 fusion.26
  5.9 1.3 %fusion.25 = (f32[4,8,4]{2,1,0:T(8,128)S(1)}, f32[4,8,4,32]{3,2,1,0:T(4,128)S(1)}) fusion(bf16[4,8,4,128]{3,2,1,0:T(4,128)(2,1)S(1)} %reshape.101, pred[4,32]{1,0:T(4,128)(4,1)S(1)} %iota_compare_fusion.3, bf16[4,32,1024]{2,1,0:T(8,128)(2,1)} %param.16), kind=kOutput, calls=%fused_computation.51 | convolution fusion | flops 1060736 | bytes 311936 | tf_op jit(solution)/shard_map/rkgd,rpkd->rkgp/dot_general | solution.py:27
  7.2 0.2 fusion.11
  7.4 0.3 multiply_reduce_fusion.1
  7.9 1.0 %convolution_convert_fusion.1 = bf16[8,2,4096]{2,0,1:T(8,128)(2,1)S(1)} fusion(bf16[4,4096]{1,0:T(4,128)(2,1)S(1)} %convert_element_type.83, f32[4096]{0:T(1024)} %param.19, f32[4]{0:T(128)S(1)} %add_rsqrt_fusion, s32[4,8,2]{1,0,2:T(4,128)S(1)} %fusion.19), kind=kOutput, calls=%fused_computation.6 | convolution fusion | flops 655424 | bytes 180496 | tf_op jit(solution)/shard_map/rec,rd->ecd/dot_general | solution.py:95
  9.0 0.9 %broadcast_in_dim.48 = bf16[8,2,2,4096]{3,2,1,0:T(2,128)(2,1)} broadcast(bf16[8,2,4096]{2,1,0:T(2,128)(2,1)S(1)} %copy.35), dimensions={0,2,3} | broadcast | bytes 393216 | tf_op jit(solution)/shard_map/broadcast_in_dim | solution.py:98
  9.9 7.4 %all-to-all-start = ((bf16[16,2,4096]{2,1,0:T(2,128)(2,1)}), bf16[16,2,4096]{2,1,0:T(2,128)(2,1)S(1)}, u32[]{:S(2)}, u32[]{:S(2)}) async-start(bf16[16,2,4096]{2,1,0:T(2,128)(2,1)} %bitcast.4), calls=%async_computation | async-start | bytes 524288 | tf_op jit(solution)/shard_map/all_to_all | solution.py:103
  17.3 0.8 convert_bitcast_fusion.1
  18.1 9.2 %all-to-all-done = bf16[16,2,4096]{2,1,0:T(2,128)(2,1)S(1)} async-done(((bf16[16,2,4096]{2,1,0:T(2,128)(2,1)}), bf16[16,2,4096]{2,1,0:T(2,128)(2,1)S(1)}, u32[]{:S(2)}, u32[]{:S(2)}) %all-to-all-start) | async-done | bytes 262176 | tf_op jit(solution)/shard_map/all_to_all | solution.py:103
  27.4 15.3 %convolution_maximum_fusion.1 = f32[32,4096]{1,0:T(8,128)S(1)} fusion(bf16[32,4096]{1,0:T(8,128)(2,1)S(1)} %reshape.106, bf16[4096,4096]{1,0:T(8,128)(2,1)} %param.23), kind=kOutput, calls=%fused_computation.2 | convolution fusion | flops 1073872896 | bytes 34340864 | tf_op jit(solution)/shard_map/dot_general | solution.py:106
  42.8 24.7 %convolution_convert_fusion = bf16[32,4096]{1,0:T(8,128)(2,1)S(1)} fusion(bf16[4096,4096]{1,0:T(8,128)(2,1)} %param.25, f32[32,4096]{1,0:T(8,128)S(1)} %convolution_maximum_fusion.1, bf16[32,4096]{1,0:T(8,128)(2,1)S(1)} %reshape.106, bf16[4096,4096]{1,0:T(8,128)(2,1)} %param.24, f32[4096]{0:T(1024)S(1)} %broadcast_bitcast_fusion), kind=kOutput, calls=%fused_computation.5 | convolution fusion | flops 2148139008 | bytes 68173824 | tf_op jit(solution)/shard_map/dot_general | solution.py:115
  67.5 0.9 %reshape.107 = bf16[16,2,4096]{2,1,0:T(2,128)(2,1)} reshape(bf16[32,4096]{1,0:T(8,128)(2,1)S(1)} %convolution_convert_fusion) | data formatting | bytes 524288 | tf_op jit(solution)/shard_map/reshape | solution.py:117
  68.4 3.5 %all-to-all-start.1 = ((bf16[16,2,4096]{2,1,0:T(2,128)(2,1)}), bf16[16,2,4096]{2,1,0:T(2,128)(2,1)S(1)}, u32[]{:S(2)}, u32[]{:S(2)}) async-start(bf16[16,2,4096]{2,1,0:T(2,128)(2,1)} %reshape.107), calls=%async_computation.1 | async-start | bytes 524288 | tf_op jit(solution)/shard_map/all_to_all | solution.py:116
  72.2 9.7 %all-to-all-done.1 = bf16[16,2,4096]{2,1,0:T(2,128)(2,1)S(1)} async-done(((bf16[16,2,4096]{2,1,0:T(2,128)(2,1)}), bf16[16,2,4096]{2,1,0:T(2,128)(2,1)S(1)}, u32[]{:S(2)}, u32[]{:S(2)}) %all-to-all-start.1) | async-done | bytes 262176 | tf_op jit(solution)/shard_map/all_to_all | solution.py:116
  81.9 0.3 convert_reduce_fusion
  82.2 0.2 mul.99
  82.4 0.9 %multiply_reduce_fusion = bf16[4,4096]{1,0:T(4,128)(2,1)} fusion(f32[16,4096]{1,0:T(8,128)S(1)} %mul.99, f32[4,16]{1,0:T(4,128)S(1)} %copy.34), kind=kLoop, calls=%fused_computation.11 | loop fusion | flops 507904 | bytes 295168 | tf_op jit(solution)/shard_map/reduce_sum | solution.py:127
  (24 shorter events, 1.1 us)
Async XLA Ops:
  0.6 6.8 %copy-start = (bf16[4,32,1024]{2,1,0:T(8,128)(2,1)S(1)}, bf16[4,32,1024]{2,1,0:T(8,128)(2,1)}, u32[]{:S(2)}) copy-start(bf16[4,32,1024]{2,1,0:T(8,128)(2,1)} %param.17) | copy-start | bytes 786436
  7.8 59.7 %copy-start.1 = (bf16[4,4096]{1,0:T(4,128)(2,1)}, bf16[4,4096]{1,0:T(4,128)(2,1)S(1)}, u32[]{:S(2)}) copy-start(bf16[4,4096]{1,0:T(4,128)(2,1)S(1)} %convert_element_type.83) | copy-start | bytes 98308
  9.9 17.4 %all-to-all-start = ((bf16[16,2,4096]{2,1,0:T(2,128)(2,1)}), bf16[16,2,4096]{2,1,0:T(2,128)(2,1)S(1)}, u32[]{:S(2)}, u32[]{:S(2)}) async-start(bf16[16,2,4096]{2,1,0:T(2,128)(2,1)} %bitcast.4), calls=%async_computation | async-start | bytes 524288 | tf_op jit(solution)/shard_map/all_to_all | solution.py:103
  42.7 29.2 %copy-start.2 = (f32[4,2]{0,1:T(2,128)S(1)}, f32[4,2]{0,1:T(2,128)}, u32[]{:S(2)}) copy-start(f32[4,2]{0,1:T(2,128)} %param.21) | copy-start | bytes 100
  68.4 13.5 %all-to-all-start.1 = ((bf16[16,2,4096]{2,1,0:T(2,128)(2,1)}), bf16[16,2,4096]{2,1,0:T(2,128)(2,1)S(1)}, u32[]{:S(2)}, u32[]{:S(2)}) async-start(bf16[16,2,4096]{2,1,0:T(2,128)(2,1)} %reshape.107), calls=%async_computation.1 | async-start | bytes 524288 | tf_op jit(solution)/shard_map/all_to_all | solution.py:116
where the time goes:
time: 84 us; the launch traced here: 83.3 us
  matrix products  42.8 us (51%)
  waiting for transfers between devices  18.9 us (22%)
  starting transfers between devices  10.9 us (13%)
  local copies, waits for them, and re-layouts  5.03 us (6%)
  other arithmetic  4.87 us (6%)
    dot_general x1, matrix products, shards(): jnp.dot(hidden, down_weight, preferred_element_type=jnp.float32)  24.7 us
    dot_general x1, matrix products, shards(): lax.dot_general(flattened, gate_weight, (((1,), (1,)), ((), ())), preferr...  15.3 us
    all_to_all x1, waiting for transfers between devices, shards(): lax.all_to_all(partial_value.astype(jnp.bfloat16).reshape(slot_rows.shape...  9.73 us
    all_to_all x1, waiting for transfers between devices, shards(): lax.all_to_all(outgoing, 'exp', split_axis=0, concat_axis=0, tiled=True)  9.18 us
    all_to_all x1, starting transfers between devices, shards(): lax.all_to_all(outgoing, 'exp', split_axis=0, concat_axis=0, tiled=True)  7.36 us
    all_to_all x1, starting transfers between devices, shards(): lax.all_to_all(partial_value.astype(jnp.bfloat16).reshape(slot_rows.shape...  3.53 us
  transfers between devices with their start and end apart: 2, of which 2 were waited for; matrix products, arithmetic and copies ran while one was open for 1% of the time, Pallas kernels for 0%

commit v1 on v0

v1 whole, which is shorter than its diff:
```python
import functools

import jax
import jax.numpy as jnp
from jax import lax
from jax.experimental import pallas as pl
from jax.experimental.pallas import tpu as pltpu
from jax.sharding import PartitionSpec as P

KV_HEADS = 8
BLOCK = 128
CAP = 2
EPSILON = 1e-05

QUAD = 4 * BLOCK
SLOTS = 12
EARLY = 6

VMEM = pltpu.VMEM
SMEM = pltpu.SMEM


def slot_of(ids_ref, row, choice):
    mine = ids_ref[row, choice]
    rank = jnp.int32(0)
    for r in range(row + 1):
        for k in range(2):
            if (r, k) < (row, choice):
                rank += (ids_ref[r, k] == mine).astype(jnp.int32)
    return mine * CAP + rank


def attend_kernel(
    lengths_ref, ids_ref, queries_ref, new_keys_ref, new_values_ref, keys_ref, values_ref, gain_ref, attended_ref, outgoing_ref
):
    rows, width = queries_ref.shape
    context = keys_ref.shape[1]
    head_size = new_keys_ref.shape[1] // KV_HEADS
    group = width // head_size // KV_HEADS
    spots = rows * context
    stack = group * rows
    scale = head_size ** (-0.5)
    query = queries_ref[...].astype(jnp.float32)
    new_key = new_keys_ref[...].astype(jnp.float32)
    new_value = new_values_ref[...].astype(jnp.float32)

    scores, owns = [], []
    for j in range(KV_HEADS):
        columns = slice(j * head_size, (j + 1) * head_size)
        heads = [query[:, (j * group + g) * head_size : (j * group + g + 1) * head_size] for g in range(group)]
        stacked = jnp.concatenate(heads, axis=0)
        keys = keys_ref[:, :, columns].reshape(spots, head_size)
        scores.append(
            lax.dot_general(
                stacked.astype(jnp.bfloat16), keys, (((1,), (1,)), ((), ())), preferred_element_type=jnp.float32
            )
        )
        own_key = jnp.concatenate([new_key[:, columns]] * group, axis=0)
        owns.append(jnp.sum(stacked * own_key, axis=1, keepdims=True))
    score = jnp.concatenate(scores, axis=0) * scale
    own = jnp.concatenate(owns, axis=0) * scale
    row_of_line = lax.broadcasted_iota(jnp.int32, score.shape, 0) % rows
    spot = lax.broadcasted_iota(jnp.int32, score.shape, 1)
    valid = jnp.zeros(score.shape, jnp.bool_)
    for r in range(rows):
        valid = valid | ((row_of_line == r) & (spot >= r * context) & (spot < r * context + lengths_ref[r]))
    score = jnp.where(valid, score, -jnp.inf)
    top = jnp.maximum(jnp.max(score, axis=1, keepdims=True), own)
    score_exp = jnp.exp(score - top)
    own_exp = jnp.exp(own - top)
    denominator = jnp.sum(score_exp, axis=1, keepdims=True) + own_exp
    prob = (score_exp / denominator).astype(jnp.bfloat16)
    own_prob = (own_exp / denominator).astype(jnp.bfloat16).astype(jnp.float32)

    pieces = []
    for j in range(KV_HEADS):
        columns = slice(j * head_size, (j + 1) * head_size)
        lines = slice(j * stack, (j + 1) * stack)
        values = values_ref[:, :, columns].reshape(spots, head_size)
        mixture = jnp.dot(prob[lines], values, preferred_element_type=jnp.float32)
        own_value = jnp.concatenate([new_value[:, columns]] * group, axis=0)
        mixture = mixture + own_prob[lines] * own_value
        pieces += [mixture[g * rows : (g + 1) * rows] for g in range(group)]
    attended = jnp.concatenate(pieces, axis=1).astype(jnp.bfloat16)
    attended_ref[...] = attended

    features = attended.astype(jnp.float32)
    mean_square = jnp.mean(features * features, axis=1, keepdims=True)
    normed = features * lax.rsqrt(mean_square + EPSILON) * gain_ref[...]
    normed = normed.astype(jnp.bfloat16).astype(jnp.float32)
    chips = outgoing_ref.shape[0]
    experts = 8
    line = lax.broadcasted_iota(jnp.int32, (experts * CAP, 1), 0)
    packed = jnp.zeros((experts * CAP, width), jnp.float32)
    for r in range(rows):
        chosen = (line == slot_of(ids_ref, r, 0)) | (line == slot_of(ids_ref, r, 1))
        packed = packed + jnp.where(chosen, normed[r : r + 1, :], 0.0)
    packed = packed.astype(jnp.bfloat16)
    for chip in range(chips):
        expert = chip // (chips // experts)
        outgoing_ref[chip] = packed[expert * CAP : (expert + 1) * CAP, :]


def list_blocks(flags_ref, list_ref, blocks):
    experts = flags_ref.shape[0]
    groups = lax.axis_size("exp") // experts
    position = lax.axis_index("exp")
    expert = position // groups
    first = (position % groups) * blocks

    def step(b, count):
        list_ref[count] = b
        return count + (flags_ref[expert, first + b] != 0).astype(jnp.int32)

    return lax.fori_loop(0, blocks, step, jnp.int32(0), unroll=min(blocks, 8))


def item_copies(item, count, list_ref, weights, ring_ref, sems):
    gate_ref, up_ref, down_ref = weights
    pairs = (count + 1) // 2
    slot = item % ring_ref.shape[0]

    def rows(position):
        return pl.ds(pl.multiple_of(list_ref[position] * BLOCK, BLOCK), BLOCK)

    def copy(source_ref, position, part):
        return pltpu.make_async_copy(
            source_ref.at[rows(position), :], ring_ref.at[slot, pl.ds(part * BLOCK, BLOCK), :], sems.at[slot, part]
        )

    def apply(act):
        @pl.when(item < pairs)
        def _():
            for s in range(2):
                @pl.when(2 * item + s < count)
                def _():
                    act(copy(gate_ref, 2 * item + s, s))
                    act(copy(up_ref, 2 * item + s, 2 + s))

        @pl.when(item >= pairs)
        def _():
            for s in range(4):
                position = 4 * (item - pairs) + s
                @pl.when(position < count)
                def _():
                    act(copy(down_ref, position, s))

    return apply


def item_count(count):
    return (count + 1) // 2 + (count + 3) // 4


def preload_kernel(flags_ref, gate_ref, up_ref, down_ref, ring_ref, list_ref, sems):
    blocks = gate_ref.shape[0] // BLOCK
    count = list_blocks(flags_ref, list_ref, blocks)
    weights = (gate_ref, up_ref, down_ref)
    early = jnp.minimum(item_count(count), EARLY)

    def start(item, carry):
        item_copies(item, count, list_ref, weights, ring_ref, sems)(lambda copy: copy.start())
        return carry

    def wait(item, carry):
        item_copies(item, count, list_ref, weights, ring_ref, sems)(lambda copy: copy.wait())
        return carry

    lax.fori_loop(0, early, start, 0)
    lax.fori_loop(0, early, wait, 0)


def experts_kernel(
    flags_ref, near_ref, far_ref, gate_ref, up_ref, down_ref, ring_in, keep_ref, give_ref, ring_ref, list_ref, x_ref, hidden_ref, total_ref, sems
):
    blocks = gate_ref.shape[0] // BLOCK
    half = near_ref.shape[0]
    count = list_blocks(flags_ref, list_ref, blocks)
    weights = (gate_ref, up_ref, down_ref)
    pairs = (count + 1) // 2
    items = item_count(count)

    def act(item, what):
        @pl.when(item < items)
        def _():
            item_copies(item, count, list_ref, weights, ring_ref, sems)(what)

    def start(item, carry):
        act(item, lambda copy: copy.start())
        return carry

    def settle(item):
        @pl.when(item >= EARLY)
        def _():
            act(item, lambda copy: copy.wait())

    lax.fori_loop(EARLY, ring_ref.shape[0], start, 0)
    x_ref[0:half, :] = near_ref[...]
    x_ref[half:, :] = far_ref[...]
    total_ref[...] = jnp.zeros_like(total_ref)

    def project(item, carry):
        settle(item)
        slot = item % ring_ref.shape[0]
        both = lax.dot_general(
            x_ref[...], ring_ref[slot], (((1,), (1,)), ((), ())), preferred_element_type=jnp.float32
        )
        hidden = jax.nn.relu(both[:, : 2 * BLOCK]) * jax.nn.relu(both[:, 2 * BLOCK :])
        neuron = lax.broadcasted_iota(jnp.int32, hidden.shape, 1)
        hidden = jnp.where(neuron < (count - 2 * item) * BLOCK, hidden, 0.0)
        hidden_ref[item] = hidden.astype(jnp.bfloat16)
        start(item + ring_ref.shape[0], 0)
        return carry

    lax.fori_loop(0, pairs, project, 0)

    @pl.when(pairs % 2 == 1)
    def _():
        hidden_ref[pairs] = jnp.zeros(hidden_ref.shape[1:], jnp.bfloat16)

    def contract(chunk, carry):
        item = pairs + chunk
        settle(item)
        slot = item % ring_ref.shape[0]
        for s in range(4):
            @pl.when(4 * chunk + s >= count)
            def _():
                ring_ref[slot, s * BLOCK : (s + 1) * BLOCK, :] = jnp.zeros((BLOCK, ring_ref.shape[2]), jnp.bfloat16)

        hidden = jnp.concatenate([hidden_ref[2 * chunk], hidden_ref[2 * chunk + 1]], axis=1)
        total_ref[...] += jnp.dot(hidden, ring_ref[slot], preferred_element_type=jnp.float32)
        start(item + ring_ref.shape[0], 0)
        return carry

    lax.fori_loop(0, items - pairs, contract, 0)
    keep_ref[...] = total_ref[0:half, :]
    give_ref[...] = total_ref[half:, :].astype(jnp.bfloat16)


def combine_kernel(ids_ref, route_weights_ref, returned_ref, out_ref):
    rows = out_ref.shape[0]
    chips = returned_ref.shape[0]
    experts = 8
    share = chips // experts
    line = lax.broadcasted_iota(jnp.int32, (rows, 1), 0)
    slots = [[slot_of(ids_ref, r, k) for k in range(2)] for r in range(rows)]
    total = jnp.zeros(out_ref.shape, jnp.float32)
    for expert in range(experts):
        value = returned_ref[expert * share].astype(jnp.float32)
        for part in range(1, share):
            value = value + returned_ref[expert * share + part].astype(jnp.float32)
        for c in range(CAP):
            weight = jnp.zeros((rows, 1), jnp.float32)
            for r in range(rows):
                for k in range(2):
                    hit = (slots[r][k] == expert * CAP + c).astype(jnp.float32)
                    weight = jnp.where(line == r, weight + hit * route_weights_ref[r, k], weight)
            total = total + weight * value[c : c + 1, :]
    out_ref[...] = total.astype(jnp.bfloat16)


def shards(
    queries,
    new_keys,
    new_values,
    cache_keys,
    cache_values,
    lengths,
    norm_gain,
    route_ids,
    route_weights,
    active_blocks,
    gate_weight,
    up_weight,
    down_weight,
):
    devices = lax.axis_size("exp")
    chips = devices // 2
    width = queries.shape[1]
    half = chips * CAP
    blocks = gate_weight.shape[0] // BLOCK
    same_core = [[2 * chip + core for chip in range(chips)] for core in range(2)]
    core_swap = [(device, device ^ 1) for device in range(devices)]
    vmem = pl.BlockSpec(memory_space=VMEM)
    smem = pl.BlockSpec(memory_space=SMEM)
    hbm = pl.BlockSpec(memory_space=pl.ANY)
    slots = min(SLOTS, (blocks + 1) // 2 + (blocks + 3) // 4)
    ring_shape = (slots, QUAD, width)

    attended, outgoing = pl.pallas_call(
        attend_kernel,
        out_shape=(
            jax.ShapeDtypeStruct(queries.shape, jnp.bfloat16),
            jax.ShapeDtypeStruct((chips, CAP, width), jnp.bfloat16),
        ),
        in_specs=[smem, smem] + [vmem] * 6,
        out_specs=(vmem, vmem),
        name="attend",
    )(lengths, route_ids, queries, new_keys, new_values, cache_keys, cache_values, norm_gain[None, :])

    def exchange(array):
        return lax.all_to_all(array, "exp", split_axis=0, concat_axis=0, tiled=True, axis_index_groups=same_core)

    ring = pl.pallas_call(
        preload_kernel,
        out_shape=pltpu.VMEM(ring_shape, jnp.bfloat16),
        in_specs=[smem, hbm, hbm, hbm],
        out_specs=vmem,
        scratch_shapes=[pltpu.SMEM((blocks,), jnp.int32), pltpu.SemaphoreType.DMA((slots, 4))],
        compiler_params=pltpu.CompilerParams(vmem_limit_bytes=2 * 2**20),
        cost_estimate=pl.CostEstimate(flops=0, transcendentals=0, bytes_accessed=EARLY * QUAD * width * 2),
        name="preload",
    )(active_blocks, gate_weight, up_weight, down_weight)

    near = exchange(outgoing).reshape(half, width)
    far = lax.ppermute(near, "exp", core_swap)

    keep, give, _ = pl.pallas_call(
        experts_kernel,
        out_shape=(
            jax.ShapeDtypeStruct((half, width), jnp.float32),
            jax.ShapeDtypeStruct((half, width), jnp.bfloat16),
            pltpu.VMEM(ring_shape, jnp.bfloat16),
        ),
        in_specs=[smem, vmem, vmem, hbm, hbm, hbm, vmem],
        out_specs=(vmem, vmem, vmem),
        scratch_shapes=[
            pltpu.SMEM((blocks,), jnp.int32),
            pltpu.VMEM((2 * half, width), jnp.bfloat16),
            pltpu.VMEM((blocks // 2 + 1, 2 * half, 2 * BLOCK), jnp.bfloat16),
            pltpu.VMEM((2 * half, width), jnp.float32),
            pltpu.SemaphoreType.DMA((slots, 4)),
        ],
        input_output_aliases={6: 2},
        compiler_params=pltpu.CompilerParams(vmem_limit_bytes=6 * 2**20 + 16 * half * width),
        name="experts",
    )(active_blocks, near, far, gate_weight, up_weight, down_weight, ring)

    from_core = lax.ppermute(give, "exp", core_swap)
    partial_value = (keep + from_core.astype(jnp.float32)).astype(jnp.bfloat16)
    returned = exchange(partial_value.reshape(chips, CAP, width))
    expert_out = pl.pallas_call(
        combine_kernel,
        out_shape=jax.ShapeDtypeStruct(queries.shape, jnp.bfloat16),
        in_specs=[smem, smem, vmem],
        out_specs=vmem,
        name="combine",
    )(route_ids, route_weights, returned)
    return attended, expert_out


def solution(mesh):
    rows = P(("dom", "exp"), None)
    return jax.shard_map(
        shards,
        mesh=mesh,
        in_specs=(
            rows,
            rows,
            rows,
            P(("dom", "exp"), None, None),
            P(("dom", "exp"), None, None),
            P(("dom", "exp")),
            P(),
            rows,
            rows,
            P("dom", None),
            P("exp", None),
            P("exp", None),
            P("exp", None),
        ),
        out_specs=(rows, rows),
        check_vma=False,
    )
```

time: 84 us -> 70.7 us (0.84)
  matrix products: 42.8 us -> 0 us
  Pallas kernels: 0 us -> 30 us
  blocking collectives: 0 us -> 14.6 us
  waiting for transfers between devices: 18.9 us -> 7.86 us
  other arithmetic: 4.87 us -> 0.98 us
    dot_general x6 -> x0, matrix products: 42.8 us -> none  [the longest x1 24.7 us: shards(): jnp.dot(hidden, down_weight, preferred_element_type=jnp.float32)]
    pallas_call x0 -> x4, Pallas kernels: none -> 30 us  [the longest x1 15.9 us: shards(): pl.pallas_call(experts_kernel, out_shape=(jax.ShapeDtypeStruct((half, wid...]
    all_to_all x0 -> x1, blocking collectives: none -> 14.6 us  [exchange(): lax.all_to_all(array, 'exp', split_axis=0, concat_axis=0, tiled=True, axi...]
    all_to_all x2 -> x1, waiting for transfers between devices: 18.9 us -> 6.66 us  [exchange(): lax.all_to_all(array, 'exp', split_axis=0, concat_axis=0, tiled=True, axi...]
    unnamed x8 -> x12, local copies, waits for them, and re-layouts: 0.79 us -> 3.99 us
    reduce_sum x6 -> x0, other arithmetic: 1.74 us -> none  [the longest x1 0.88 us: shards(): jnp.sum(weighted.reshape(weighted.shape[0], -1, model_width), axis=1)]
    reshape x4 -> x2, local copies, waits for them, and re-layouts: 2.49 us -> 0.8 us  [the longest x1 0.75 us: shards(): returned = exchange(partial_value.reshape(chips, CAP, width))]
    ppermute x0 -> x2, waiting for transfers between devices: none -> 1.2 us  [the longest x1 1.2 us: shards(): from_core = lax.ppermute(give, 'exp', core_swap)]
  transfers between devices with their start and end apart: 2 -> 3, of which waited for: 2 -> 2; matrix products, arithmetic and copies ran while one was open for 1% -> 1% of each run, Pallas kernels for 0% -> 13%
where the time goes in v1:
time: 70.7 us; the launch traced here: 69.9 us
  Pallas kernels  30 us (42%)
  blocking collectives  14.6 us (21%)
  starting transfers between devices  11 us (16%)
  waiting for transfers between devices  7.86 us (11%)
  local copies, waits for them, and re-layouts  4.78 us (7%)
  other arithmetic  0.98 us (1%)
  between operations  0.72 us (1%)
    pallas_call x1, Pallas kernels, shards(): pl.pallas_call(experts_kernel, out_shape=(jax.ShapeDtypeStruct((half, wid...  15.9 us
    all_to_all x1, blocking collectives, exchange(): lax.all_to_all(array, 'exp', split_axis=0, concat_axis=0, tiled=True, axi...  14.6 us
    all_to_all x1, starting transfers between devices, exchange(): lax.all_to_all(array, 'exp', split_axis=0, concat_axis=0, tiled=True, axi...  10.3 us
    pallas_call x1, Pallas kernels, shards(): pl.pallas_call(preload_kernel, out_shape=pltpu.VMEM(ring_shape, jnp.bfloa...  9.42 us
    all_to_all x1, waiting for transfers between devices, exchange(): lax.all_to_all(array, 'exp', split_axis=0, concat_axis=0, tiled=True, axi...  6.66 us
    unnamed x12, local copies, waits for them, and re-layouts  3.99 us
    pallas_call x1, Pallas kernels, shards(): pl.pallas_call(attend_kernel, out_shape=(jax.ShapeDtypeStruct(queries.sha...  2.69 us
    pallas_call x1, Pallas kernels, shards(): pl.pallas_call(combine_kernel, out_shape=jax.ShapeDtypeStruct(queries.sha...  1.97 us
  transfers between devices with their start and end apart: 3, of which 2 were waited for; matrix products, arithmetic and copies ran while one was open for 1% of the time, Pallas kernels for 13%

profile of v1, /device:TPU:0, one launch (start us, length us, event | category | flops | bytes accessed | tf_op | source)
XLA Modules:
  0.0 69.9 jit_solution(2343806499092110539)
XLA Ops:
  0.6 1.3 %copy.16.ids_ref = s32[4,2]{1,0:T(4,128)} copy(s32[4,2]{0,1:T(2,128)} %param.20) | data formatting | bytes 64 | tf_op args[7]
  2.0 2.7 %attend.1 = (bf16[4,4096]{1,0:T(4,128)(2,1)}, bf16[8,2,4096]{2,1,0:T(2,128)(2,1)}) custom-call(s32[4]{0:T(128)} %lengths_ref.1, s32[4,2]{1,0:T(4,128)} %copy.16.ids_ref, bf16[4,4096]{1,0:T(4,128)(2,1)} %queries_ref.1, bf16[4,1024]{1,0:T(4,128)(2,1)} %new_keys_ref.1, bf16[4,1024]{1,0:T(4,128)(2,1)} %new_values_ref.1, bf16[4,32,1024]{2,1,0:T(8,128)(2,1)} %keys_ref.1, ...), custom_call_target="tpu_custom_call" | custom-call | tf_op jit(solution)/shard_map/attend/pallas_call | solution.py:290
  4.7 14.6 %all_to_all.10 = bf16[8,2,4096]{2,1,0:T(2,128)(2,1)S(1)} all-to-all(bf16[8,2,4096]{2,1,0:T(2,128)(2,1)} %get-tuple-element.7), channel_id=1, replica_groups={{0,2,4,6,8,10,12,14},{1,3,5,7,9,11,13,15},{16,18,20,22,24,26,28,30},{17..., dimensions={0} | all-to-all | bytes 262144 | tf_op jit(solution)/shard_map/all_to_all | solution.py:302
  19.2 0.1 reshape.10.near_ref
  19.3 0.0 copy-start.2
  19.3 0.1 collective-permute-start
  19.4 0.0 copy-start
  19.4 0.7 copy-done
  20.1 9.4 %preload.1.ring_in = bf16[12,512,4096]{2,1,0:T(8,128)(2,1)S(1)} custom-call(s32[8,64]{1,0:T(8,128)S(1)} %copy-done, bf16[4096,4096]{1,0:T(8,128)(2,1)} %gate_ref.3, bf16[4096,4096]{1,0:T(8,128)(2,1)} %up_ref.3, bf16[4096,4096]{1,0:T(8,128)(2,1)} %down_ref.3), custom_call_target="tpu_custom_call" | custom-call | bytes 25165824 | tf_op jit(solution)/shard_map/preload/pallas_call | solution.py:304
  29.5 0.0 copy-done.2
  29.5 0.0 copy-start.4
  29.5 0.0 collective-permute-done.far_ref
  29.5 0.0 copy-start.3
  29.6 0.6 copy-done.3
  30.2 15.9 %experts.1 = (f32[16,4096]{1,0:T(8,128)}, bf16[16,4096]{1,0:T(8,128)(2,1)}, bf16[12,512,4096]{2,1,0:T(8,128)(2,1)S(1)}) custom-call(s32[8,64]{1,0:T(8,128)} %flags_ref.3, bf16[16,4096]{1,0:T(8,128)(2,1)} %copy-done.2, bf16[16,4096]{1,0:T(8,128)(2,1)} %copy-done.3, bf16[4096,4096]{1,0:T(8,128)(2,1)} %gate_ref.3, ...), custom_call_target="tpu_custom_call", output_to_operand_aliasing={{2}: (6, {})} | custom-call | tf_op jit(solution)/shard_map/experts/pallas_call | solution.py:318
  46.1 0.6 collective-permute-start.1
  46.7 1.2 %collective-permute-done.1 = bf16[16,4096]{1,0:T(8,128)(2,1)S(1)} collective-permute-done((bf16[16,4096]{1,0:T(8,128)(2,1)}, bf16[16,4096]{1,0:T(8,128)(2,1)S(1)}, u32[]{:S(2)}, u32[]{:S(2)}) %collective-permute-start.1) | collective-permute-done | bytes 131104 | tf_op jit(solution)/shard_map/ppermute | solution.py:339
  47.9 1.0 %add_convert_fusion = bf16[16,4096]{1,0:T(8,128)(2,1)S(1)} fusion(f32[16,4096]{1,0:T(8,128)} %get-tuple-element.8, bf16[16,4096]{1,0:T(8,128)(2,1)S(1)} %collective-permute-done.1), kind=kLoop, calls=%fused_computation | loop fusion | flops 196608 | bytes 524288 | tf_op jit(solution)/shard_map/convert_element_type | solution.py:340
  48.9 0.7 %reshape.11 = bf16[8,2,4096]{2,1,0:T(2,128)(2,1)} reshape(bf16[16,4096]{1,0:T(8,128)(2,1)S(1)} %add_convert_fusion) | data formatting | bytes 262144 | tf_op jit(solution)/shard_map/reshape | solution.py:341
  49.6 10.3 %all-to-all-start.1 = ((bf16[8,2,4096]{2,1,0:T(2,128)(2,1)}), bf16[8,2,4096]{2,1,0:T(2,128)(2,1)S(1)}, u32[]{:S(2)}, u32[]{:S(2)}) async-start(bf16[8,2,4096]{2,1,0:T(2,128)(2,1)} %reshape.11), calls=%async_computation.1 | async-start | bytes 262144 | tf_op jit(solution)/shard_map/all_to_all | solution.py:302
  60.0 0.7 copy.18.route_weights_ref
  60.6 6.7 %all-to-all-done.1.returned_ref = bf16[8,2,4096]{2,1,0:T(2,128)(2,1)S(1)} async-done(((bf16[8,2,4096]{2,1,0:T(2,128)(2,1)}), bf16[8,2,4096]{2,1,0:T(2,128)(2,1)S(1)}, u32[]{:S(2)}, u32[]{:S(2)}) %all-to-all-start.1) | async-done | bytes 131104 | tf_op jit(solution)/shard_map/all_to_all | solution.py:302
  67.3 0.6 copy-done.1
  67.9 2.0 %combine.1 = bf16[4,4096]{1,0:T(4,128)(2,1)} custom-call(s32[4,2]{1,0:T(4,128)} %copy.16.ids_ref, f32[4,2]{1,0:T(4,128)} %copy.18.route_weights_ref, bf16[8,2,4096]{2,1,0:T(2,128)(2,1)} %copy-done.1), custom_call_target="tpu_custom_call" | custom-call | tf_op jit(solution)/shard_map/combine/pallas_call | solution.py:342
  (2 shorter events, 0.0 us)
Async XLA Ops:
  19.3 10.2 %copy-start.2 = (bf16[16,4096]{1,0:T(8,128)(2,1)}, bf16[16,4096]{1,0:T(8,128)(2,1)S(1)}, u32[]{:S(2)}) copy-start(bf16[16,4096]{1,0:T(8,128)(2,1)S(1)} %reshape.10.near_ref) | copy-start | bytes 393220
  19.3 10.2 %collective-permute-start = (bf16[16,4096]{1,0:T(8,128)(2,1)S(1)}, bf16[16,4096]{1,0:T(8,128)(2,1)S(1)}, u32[]{:S(2)}, u32[]{:S(2)}) collective-permute-start(bf16[16,4096]{1,0:T(8,128)(2,1)S(1)} %reshape.10.near_ref), channel_id=1, source_target_pairs={{0,1},{1,0},{2,3},{3,2},{4,5},{5,4},{6,7},{7,6},{8,9},{9,8},{10,11... | collective-permute-start | bytes 393224 | tf_op jit(solution)/shard_map/ppermute | solution.py:316
  19.4 0.7 copy-start
  29.5 30.4 %copy-start.4 = (f32[4,2]{0,1:T(2,128)S(1)}, f32[4,2]{0,1:T(2,128)}, u32[]{:S(2)}) copy-start(f32[4,2]{0,1:T(2,128)} %param.21) | copy-start | bytes 100
  29.5 0.6 copy-start.3
  46.1 1.8 %collective-permute-start.1 = (bf16[16,4096]{1,0:T(8,128)(2,1)}, bf16[16,4096]{1,0:T(8,128)(2,1)S(1)}, u32[]{:S(2)}, u32[]{:S(2)}) collective-permute-start(bf16[16,4096]{1,0:T(8,128)(2,1)} %get-tuple-element.9), channel_id=1, source_target_pairs={{0,1},{1,0},{2,3},{3,2},{4,5},{5,4},{6,7},{7,6},{8,9},{9,8},{10,11... | collective-permute-start | bytes 393224 | tf_op jit(solution)/shard_map/ppermute | solution.py:339
  49.6 17.7 %all-to-all-start.1 = ((bf16[8,2,4096]{2,1,0:T(2,128)(2,1)}), bf16[8,2,4096]{2,1,0:T(2,128)(2,1)S(1)}, u32[]{:S(2)}, u32[]{:S(2)}) async-start(bf16[8,2,4096]{2,1,0:T(2,128)(2,1)} %reshape.11), calls=%async_computation.1 | async-start | bytes 262144 | tf_op jit(solution)/shard_map/all_to_all | solution.py:302
  67.3 0.6 copy-start.1
